TPU v7x, 128 devices: a whole 4x4x4 slice. The times are simulated.
128 devices in a mesh: dp: 2 (over core), expert: 8 (over x, z_lo), tensor: 8 (over y, z_hi).
Axes of the slice: x: 4, y: 4, z: 4 (z_hi: 2, z_lo: 2; z = z_hi * 2 + z_lo), core: 2. Of those that a mesh axis runs over, the one named last changes fastest.
Arguments:
- tokens: bfloat16 [512, 5120], P(('dp', 'expert'), 'tensor'), may hold values from -50 to 50
- expert_ids: int32 [512, 2], P(('dp', 'expert')), may hold values from 0 to 7, all different within a row; in each aligned block of 32 rows (0 to 31, 32 to 63, ...) at most 16 rows name the same one
- gate_weights: float32 [512, 2], P(('dp', 'expert')), may hold values from 0.1 to 1
- t_gate: bfloat16 [8, 5120, 8192], P('expert', None, ('dp', 'tensor')), may hold values from -0.078125 to 0.078125
- t_up: bfloat16 [8, 5120, 8192], P('expert', None, ('dp', 'tensor')), may hold values from -0.078125 to 0.078125
- t_down: bfloat16 [8, 8192, 5120], P('expert', ('dp', 'tensor')), may hold values from -0.09375 to 0.09375
- s_gate: bfloat16 [5120, 8192], P(None, ('expert', 'tensor')), may hold values from -0.078125 to 0.078125
- s_up: bfloat16 [5120, 8192], P(None, ('expert', 'tensor')), may hold values from -0.078125 to 0.078125
- s_down: bfloat16 [8192, 5120], P(('expert', 'tensor')), may hold values from -0.1875 to 0.1875
Outputs:
- grad_gate: bfloat16 [5120, 8192], P(None, ('expert', 'tensor'))
- grad_up: bfloat16 [5120, 8192], P(None, ('expert', 'tensor'))
- grad_down: bfloat16 [8192, 5120], P(('expert', 'tensor'))
- loss: float32 [], replicated
Inputs may be any that keep to these rules, and one draw needn't show every extreme that they name: `expert_ids`: in each aligned block of 32 tokens no expert is named by more than 16 tokens; a token's two experts differ.
All inputs are finite; a program needn't handle non-finite values.
Results may differ from a plain program's by a relative error of at most 0.018.
Values may be sent and summed in bfloat16 or wider, within the bound.
A program may use at most 128 MiB of HBM per device.

v0:
```python
import functools
import math

import jax
import jax.numpy as jnp
from jax import lax
from jax.sharding import Mesh
from jax.sharding import PartitionSpec as P

EXPERT = ("expert_0", "expert_1")
TENSOR = ("tensor_0", "tensor_1")
DP_TENSOR = ("dp", "tensor_0", "tensor_1")
DP_EXPERT_TENSOR = ("dp", "expert_0", "expert_1", "tensor_0", "tensor_1")
EXPERT_TENSOR = ("expert_0", "expert_1", "tensor_0", "tensor_1")
DP_EXPERT = ("dp", "expert_0", "expert_1")


def joined_along(pieces, dim):
    pieces = jnp.moveaxis(pieces, 0, dim)
    lengths = pieces.shape
    return pieces.reshape(*lengths[:dim], lengths[dim] * lengths[dim + 1], *lengths[dim + 2 :])


def sent_to_all(array, axis):
    copies = jnp.broadcast_to(array, (lax.axis_size(axis), *array.shape))
    return lax.all_to_all(copies, axis, split_axis=0, concat_axis=0, tiled=True)


def gathered_copies(array, axis, dim):
    return joined_along(sent_to_all(array, axis), dim)


def summed_rows(array, axes, dim):
    if not axes:
        return array
    nearer = lax.psum_scatter(array, axes[0], scatter_dimension=dim, tiled=True)
    return summed_rows(nearer, axes[1:], dim)


def in_blocks(array, dim, peers):
    lengths = array.shape
    pieces = array.reshape(*lengths[:dim], peers, lengths[dim] // peers, *lengths[dim + 1 :])
    return jnp.moveaxis(pieces, dim, 0)


def sent_and_summed(array, axis, dim):
    peers = lax.axis_size(axis)
    pieces = lax.all_to_all(in_blocks(array, dim, peers), axis, 0, 0, tiled=True)
    return jnp.sum(pieces.astype(jnp.float32), axis=0)


def by_axis(array, axes):
    return functools.reduce(lax.psum, axes, array)


def over_pieces(array, axis):
    return lax.all_gather(array, axis).astype(jnp.float32).sum(0)


def pair_slots(route_ids, experts, capacity):
    flat_ids = route_ids.reshape(-1)
    onehot = (flat_ids[:, None] == jnp.arange(experts, dtype=jnp.int32)[None, :]).astype(jnp.int32)
    before = jnp.cumsum(onehot, axis=0) - onehot
    slot_rank = jnp.sum(before * onehot, axis=1)
    return (flat_ids * capacity + slot_rank).reshape(route_ids.shape)


def body(tokens, expert_ids, gate_weights, t_gate, t_up, t_down, s_gate, s_up, s_down):
    experts = lax.axis_size(EXPERT)
    tensor_count = lax.axis_size(TENSOR)
    data_count = lax.axis_size("dp")
    group_rows = tokens.shape[0]
    slice_width = tokens.shape[1]
    model_width = slice_width * tensor_count
    capacity = 4 * group_rows // experts
    pair_codes = pair_slots(expert_ids, experts, capacity)
    slot_codes = jnp.arange(experts * capacity, dtype=jnp.int32)
    placing = jnp.sum(
        (pair_codes[None, :, :] == slot_codes[:, None, None]).astype(jnp.float32), axis=2
    ).astype(jnp.bfloat16)
    full_rows = gathered_copies(tokens, TENSOR, 1)
    sent = jnp.dot(placing, full_rows, preferred_element_type=jnp.float32).astype(jnp.bfloat16)
    sent = sent.reshape(experts, capacity, model_width)
    received = lax.all_to_all(sent, EXPERT, split_axis=0, concat_axis=0, tiled=True)
    slot_rows = received.reshape(experts * capacity, model_width)
    shard_rows = gathered_copies(slot_rows, "dp", 0)
    gate_pre = jnp.dot(shard_rows, t_gate[0], preferred_element_type=jnp.float32)
    up_pre = jnp.dot(shard_rows, t_up[0], preferred_element_type=jnp.float32)
    teacher_act = (gate_pre * jax.nn.sigmoid(gate_pre) * up_pre).astype(jnp.bfloat16)
    hidden_local = teacher_act.shape[1]
    slot_total = experts * capacity
    teacher_part = jnp.einsum(
        "dqf,ftc->dtqc",
        teacher_act.reshape(data_count, slot_total, hidden_local),
        t_down[0].reshape(hidden_local, tensor_count, slice_width),
        preferred_element_type=jnp.float32,
    )
    teacher_part = teacher_part.reshape(data_count * tensor_count * slot_total, slice_width)
    expert_out = lax.psum_scatter(
        teacher_part.astype(jnp.bfloat16), DP_TENSOR, scatter_dimension=0, tiled=True
    )
    back = lax.all_to_all(
        expert_out.reshape(experts, capacity, slice_width),
        EXPERT,
        split_axis=0,
        concat_axis=0,
        tiled=True,
    )
    weighting = gate_weights / jnp.sum(gate_weights, axis=1, keepdims=True)
    mixing = jnp.sum(
        weighting[:, :, None]
        * (pair_codes[:, :, None] == slot_codes[None, None, :]).astype(jnp.float32),
        axis=1,
    )
    teacher_out = jnp.dot(
        mixing,
        back.reshape(slot_total, slice_width).astype(jnp.float32),
        precision=lax.Precision.HIGHEST,
    )
    group_x = gathered_copies(full_rows, EXPERT, 0)
    gate_pre = jnp.dot(group_x, s_gate, preferred_element_type=jnp.float32)
    up_pre = jnp.dot(group_x, s_up, preferred_element_type=jnp.float32)
    gate_sig = jax.nn.sigmoid(gate_pre)
    activation = (gate_pre * gate_sig * up_pre).astype(jnp.bfloat16)
    student_local = activation.shape[1]
    act_split = activation.reshape(experts, group_rows, student_local)
    down_split = s_down.reshape(student_local, tensor_count, slice_width)
    partial_value = jnp.dot(activation, s_down, preferred_element_type=jnp.float32)
    column_part = summed_rows(partial_value.astype(jnp.bfloat16), TENSOR, 1).astype(jnp.float32)
    student_out = sent_and_summed(column_part.astype(jnp.bfloat16), EXPERT, 0)
    residual = student_out - teacher_out
    total_tokens = group_rows * experts * data_count
    loss_total = by_axis(jnp.sum(residual * residual), DP_EXPERT_TENSOR)
    loss_value = loss_total / (total_tokens * model_width)
    grad_scale = 1.0 / math.sqrt(total_tokens)
    d_out = (residual * grad_scale).astype(jnp.bfloat16)
    gathered = lax.all_gather(d_out, EXPERT_TENSOR, axis=0, tiled=True)
    gathered = gathered.reshape(experts, tensor_count, group_rows, slice_width)
    d_act = jnp.einsum("etrc,ftc->erf", gathered, down_split, preferred_element_type=jnp.float32)
    d_act = d_act.reshape(experts * group_rows, student_local)
    d_down = jnp.einsum("erf,etrc->ftc", act_split, gathered, preferred_element_type=jnp.float32)
    d_down = d_down.reshape(student_local, model_width)
    d_gate_pre = (d_act * up_pre * gate_sig * (1.0 + gate_pre * (1.0 - gate_sig))).astype(
        jnp.bfloat16
    )
    d_up_pre = (d_act * gate_pre * gate_sig).astype(jnp.bfloat16)
    d_gate = jnp.einsum("rd,rf->df", group_x, d_gate_pre, preferred_element_type=jnp.float32)
    d_up = jnp.einsum("rd,rf->df", group_x, d_up_pre, preferred_element_type=jnp.float32)
    grad_sums = (
        over_pieces(d_gate.astype(jnp.bfloat16), "dp").astype(jnp.float32),
        over_pieces(d_up.astype(jnp.bfloat16), "dp").astype(jnp.float32),
        over_pieces(d_down.astype(jnp.bfloat16), "dp").astype(jnp.float32),
    )
    return (
        grad_sums[0].astype(jnp.bfloat16),
        grad_sums[1].astype(jnp.bfloat16),
        grad_sums[2].astype(jnp.bfloat16),
        loss_value,
    )


def solution(mesh):
    finer = Mesh(
        mesh.devices.reshape(mesh.shape["dp"], 4, 2, 4, 2),
        ("dp", "expert_0", "expert_1", "tensor_0", "tensor_1"),
    )
    placed = (
        P(DP_EXPERT, TENSOR),
        P(DP_EXPERT, None),
        P(DP_EXPERT, None),
        P(EXPERT, None, DP_TENSOR),
        P(EXPERT, None, DP_TENSOR),
        P(EXPERT, DP_TENSOR, None),
        P(None, EXPERT_TENSOR),
        P(None, EXPERT_TENSOR),
        P(EXPERT_TENSOR, None),
    )
    return jax.shard_map(
        body,
        mesh=finer,
        in_specs=placed,
        out_specs=(P(None, EXPERT_TENSOR), P(None, EXPERT_TENSOR), P(EXPERT_TENSOR, None), P()),
        check_vma=False,
    )
```

profile of v0, /device:TPU:1, one launch (start us, length us, event | category | flops | bytes accessed | tf_op | source)
XLA Modules:
  0.0 624.2 jit_solution(16759857496306877032)
XLA Ops:
  7.2 0.9 broadcast_in_dim.6
  8.1 16.5 %all_to_all.30 = bf16[8,32,640]{2,1,0:T(8,128)(2,1)S(1)} all-to-all(bf16[8,32,640]{2,1,0:T(8,128)(2,1)S(1)} %broadcast_in_dim.6), channel_id=1, replica_groups=mesh['dp'=2,'expert_0'=4,'expert_1'=2,'tensor_0'=4,'tensor_1'=2] {'tenso..., dimensions={0} | all-to-all | bytes 655360 | tf_op jit(solution)/shard_map/all_to_all | solution.py:26
  24.6 0.3 broadcast_in_dim.7
  24.9 34.3 %all_to_all.31 = bf16[8,32,5120]{2,1,0:T(8,128)(2,1)S(1)} all-to-all(bf16[8,32,5120]{2,1,0:T(8,128)(2,1)S(1)} %broadcast_in_dim.7), channel_id=1, replica_groups=mesh['dp'=2,'expert_0'=4,'expert_1'=2,'tensor_0'=4,'tensor_1'=2] {'exper..., dimensions={0} | all-to-all | bytes 5242880 | tf_op jit(solution)/shard_map/all_to_all | solution.py:26
  59.3 0.8 fusion.31
  60.1 0.8 multiply_convert_fusion.2
  61.0 0.5 copy-done.5
  61.5 2.4 convolution_convert_fusion
  64.3 0.2 select_reduce_fusion.1
  64.7 1.6 convolution_convert_fusion.3
  66.3 3.6 all-to-all-start.3
  69.9 6.1 copy.67
  76.0 10.1 %all-to-all-done.3 = bf16[8,16,5120]{2,1,0:T(8,128)(2,1)S(1)} async-done(((bf16[8,16,5120]{2,1,0:T(8,128)(2,1)}), bf16[8,16,5120]{2,1,0:T(8,128)(2,1)S(1)}, u32[]{:S(2)}, u32[]{:S(2)}) %all-to-all-start.3) | async-done | bytes 1310752 | tf_op jit(solution)/shard_map/all_to_all | solution.py:84
  86.1 1.8 broadcast_in_dim.16
  87.9 7.3 %all-to-all-start.4 = ((bf16[2,128,5120]{2,1,0:T(8,128)(2,1)}), bf16[2,128,5120]{2,1,0:T(8,128)(2,1)S(1)}, u32[]{:S(2)}, u32[]{:S(2)}) async-start(bf16[2,128,5120]{2,1,0:T(8,128)(2,1)} %broadcast_in_dim.16), calls=%async_computation.5 | async-start | bytes 5242880 | tf_op jit(solution)/shard_map/all_to_all | solution.py:26
  95.2 2.2 reduce-scatter.6.cloned.1.call-done
  97.4 2.2 copy.62
  99.7 4.1 fusion.7
  103.8 4.1 fusion.19
  108.0 3.5 fusion.10
  111.5 8.7 %reduce-scatter.10.cloned.1.call-done = bf16[640,256]{1,0:T(8,128)(2,1)} async-done(((bf16[1280,256]{1,0:T(8,128)(2,1)}), bf16[640,256]{1,0:T(8,128)(2,1)}) %reduce-scatter.10.cloned.1.call-update) | async-done | bytes 327696
  120.2 1.9 copy.63
  122.1 4.1 all-to-all-start.2
  126.2 69.8 %reduce-scatter.8.cloned.1.call-done = bf16[128,640]{1,0:T(8,128)(2,1)} async-done(((bf16[2048,640]{1,0:T(8,128)(2,1)}), bf16[128,640]{1,0:T(8,128)(2,1)}) %reduce-scatter.8.cloned.1.call-update) | async-done | bytes 163856 | tf_op jit(solution)/shard_map/reduce_scatter | solution.py:99
  196.0 3.8 all-to-all-start.5
  200.0 5.2 all-to-all-done.5
  205.2 1.4 multiply_reduce_fusion
  206.7 291.1 %all-gather.8.cloned.1.call-done = bf16[2048,640]{1,0:T(8,128)(2,1)} async-done(((bf16[32,640]{1,0:T(8,128)(2,1)}), bf16[2048,640]{1,0:T(8,128)(2,1)}) %all-gather.8.cloned.1.call-update) | async-done | bytes 2621456 | tf_op jit(solution)/shard_map/all_gather | solution.py:137
  497.8 2.1 copy.56
  499.9 0.8 fusion.22
  500.8 0.9 copy-done.3
  501.7 1.7 fusion.1
  503.3 0.2 all-gather.14.cloned.1.call-start
  503.6 2.1 copy.66
  505.7 1.7 fusion
  507.5 1.6 fusion.2
  509.1 47.5 %psum.35 = f32[]{:T(128)} all-reduce(f32[]{:T(128)} %get-tuple-element.16), channel_id=1, replica_groups=mesh['dp'=2,'expert_0'=4,'expert_1'=2,'tensor_0'=4,'tensor_1'=2] {'dp'}, use_global_device_ids=true, to_apply=%region_13.14 | all-reduce | flops 1 | bytes 8 | tf_op jit(solution)/shard_map/psum | solution.py:53
  556.6 6.7 %psum.36 = f32[]{:T(128)} all-reduce(f32[]{:T(128)} %psum.35), channel_id=1, replica_groups=mesh['dp'=2,'expert_0'=4,'expert_1'=2,'tensor_0'=4,'tensor_1'=2] {'exper..., use_global_device_ids=true, to_apply=%region_14.15 | all-reduce | flops 1 | bytes 8 | tf_op jit(solution)/shard_map/psum | solution.py:53
  563.3 4.4 psum.37
  567.7 9.5 %psum.38 = f32[]{:T(128)} all-reduce(f32[]{:T(128)} %psum.37), channel_id=1, replica_groups=mesh['dp'=2,'expert_0'=4,'expert_1'=2,'tensor_0'=4,'tensor_1'=2] {'tenso..., use_global_device_ids=true, to_apply=%region_16.17 | all-reduce | flops 1 | bytes 8 | tf_op jit(solution)/shard_map/psum | solution.py:53
  577.2 5.9 psum.39
  583.8 3.7 reshape.78
  587.5 8.1 %reduce_sum.98 = bf16[5120,128]{0,1:T(8,128)(2,1)} reduce(bf16[2,5120,128]{1,0,2:T(2,128)(2,1)S(1)} %reshape.78, bf16[]{:T(256)} %constant.21.clone.1), dimensions={0}, to_apply=%region_9.10 | reduce | flops 655360 | bytes 3932162 | tf_op jit(solution)/shard_map/reduce_sum | solution.py:57
  595.6 2.4 copy.59
  598.0 3.7 reduce_sum.100
  601.7 5.0 reshape.79
  606.6 8.1 %reduce_sum.99 = bf16[5120,128]{0,1:T(8,128)(2,1)S(1)} reduce(bf16[2,5120,128]{1,0,2:T(2,128)(2,1)} %reshape.79, bf16[]{:T(256)} %constant.21.clone.1), dimensions={0}, to_apply=%region_10.11 | reduce | flops 655360 | bytes 3932162 | tf_op jit(solution)/shard_map/reduce_sum | solution.py:57
  614.7 1.4 copy.60
  (52 shorter events, 1.2 us)
Async XLA Ops:
  7.2 52.9 %copy-start = (bf16[5120,128]{1,0:T(8,128)(2,1)S(1)}, bf16[5120,128]{1,0:T(8,128)(2,1)}, u32[]{:S(2)}) copy-start(bf16[5120,128]{1,0:T(8,128)(2,1)} %param.16) | copy-start | bytes 3932164
  7.2 90.2 %reduce-scatter.6.cloned.1.call-start = ((), (), s32[]{:S(2)}) async-start(), calls=%async_computation.9 | async-start | bytes 3276800 | tf_op jit(solution)/shard_map/reduce_scatter | solution.py:36
  24.9 34.3 %copy-start.4 = (bf16[5120,128]{1,0:T(8,128)(2,1)S(1)}, bf16[5120,128]{1,0:T(8,128)(2,1)}, u32[]{:S(2)}) copy-start(bf16[5120,128]{1,0:T(8,128)(2,1)} %param.15) | copy-start | bytes 3932164
  59.3 1.7 copy-start.2
  60.1 1.4 copy-start.5
  61.5 2.4 copy-start.7
  66.3 19.8 %all-to-all-start.3 = ((bf16[8,16,5120]{2,1,0:T(8,128)(2,1)}), bf16[8,16,5120]{2,1,0:T(8,128)(2,1)S(1)}, u32[]{:S(2)}, u32[]{:S(2)}) async-start(bf16[8,16,5120]{2,1,0:T(8,128)(2,1)} %bitcast.3), calls=%async_computation.4 | async-start | bytes 2621440 | tf_op jit(solution)/shard_map/all_to_all | solution.py:84
  87.9 11.7 %all-to-all-start.4 = ((bf16[2,128,5120]{2,1,0:T(8,128)(2,1)}), bf16[2,128,5120]{2,1,0:T(8,128)(2,1)S(1)}, u32[]{:S(2)}, u32[]{:S(2)}) async-start(bf16[2,128,5120]{2,1,0:T(8,128)(2,1)} %broadcast_in_dim.16), calls=%async_computation.5 | async-start | bytes 5242880 | tf_op jit(solution)/shard_map/all_to_all | solution.py:26
  95.2 25.0 %reduce-scatter.10.cloned.1.call-start = ((), (), s32[]{:S(2)}) async-start(), calls=%async_computation.15 | async-start | bytes 983040
  99.6 96.4 %reduce-scatter.8.cloned.1.call-start = ((), (), s32[]{:S(2)}) async-start(), calls=%async_computation.10 | async-start | bytes 2785280 | tf_op jit(solution)/shard_map/reduce_scatter | solution.py:99
  99.6 8.3 %slice-start = ((s8[5242880]{0:T(1024)(128)(4,1)}), s8[4194304]{0:T(1024)(128)(4,1)S(1)}, s32[]{:S(2)}) async-start(s8[5242880]{0:T(1024)(128)(4,1)} %bitcast.94), calls=%async_computation.16 | async-start | bytes 8388608
  103.8 4.1 slice-start.1
  111.5 14.7 %copy-start.8 = (f32[32,2]{0,1:T(2,128)S(1)}, f32[32,2]{0,1:T(2,128)}, u32[]{:S(2)}) copy-start(f32[32,2]{0,1:T(2,128)} %param.11) | copy-start | bytes 772
  122.1 73.9 %all-to-all-start.2 = ((bf16[8,32,640]{2,1,0:T(8,128)(2,1)}), bf16[8,32,640]{2,1,0:T(8,128)(2,1)S(1)}, u32[]{:S(2)}, u32[]{:S(2)}) async-start(bf16[8,32,640]{2,1,0:T(8,128)(2,1)} %bitcast.2), calls=%async_computation.3 | async-start | bytes 655360 | tf_op jit(solution)/shard_map/all_to_all | solution.py:48
  196.0 9.2 %all-to-all-start.5 = ((bf16[8,16,640]{2,1,0:T(8,128)(2,1)}), bf16[8,16,640]{2,1,0:T(8,128)(2,1)S(1)}, u32[]{:S(2)}, u32[]{:S(2)}) async-start(bf16[8,16,640]{2,1,0:T(8,128)(2,1)} %bitcast.111), calls=%async_computation.7 | async-start | bytes 327680 | tf_op jit(solution)/shard_map/all_to_all | solution.py:102
  199.8 298.0 %all-gather.8.cloned.1.call-start = ((), (), s32[]{:S(2)}) async-start(), calls=%async_computation.11 | async-start | bytes 2662400 | tf_op jit(solution)/shard_map/all_gather | solution.py:137
  206.6 377.2 %all-gather.10.cloned.1.call-start = ((), (), s32[]{:S(2)}) async-start(), calls=%async_computation.12 | async-start | bytes 3932160 | tf_op jit(solution)/shard_map/all_gather | solution.py:57
  497.8 2.1 copy-start.6
  499.9 1.7 copy-start.3
  503.3 94.6 %all-gather.14.cloned.1.call-start = ((), (), s32[]{:S(2)}) async-start(), calls=%async_computation.14 | async-start | bytes 3932160 | tf_op jit(solution)/shard_map/all_gather | solution.py:57
  507.4 94.2 %all-gather.12.cloned.1.call-start = ((), (), s32[]{:S(2)}) async-start(), calls=%async_computation.13 | async-start | bytes 3932160 | tf_op jit(solution)/shard_map/all_gather | solution.py:57
  601.7 14.5 %copy-start.1 = (bf16[5120,128]{1,0:T(8,128)(2,1)S(1)}, bf16[5120,128]{1,0:T(8,128)(2,1)}, u32[]{:S(2)}) copy-start(bf16[5120,128]{1,0:T(8,128)(2,1)} %param.16) | copy-start | bytes 3932164
Sparse Core Ops, SparseCore 0:
  64.0 33.3 reduce-scatter.5
  100.3 19.8 reduce-scatter.9
  124.7 71.2 reduce-scatter.7
  206.7 291.0 all-gather.7
  503.5 56.4 all-gather.9
  561.5 15.3 all-gather.13
  579.2 15.3 all-gather.11
where the time goes:
time: 630 us; the launch traced here: 624 us
  waiting for transfers between devices  387 us (61%)
  blocking collectives  125 us (20%)
  local copies, waits for them, and re-layouts  31.7 us (5%)
  matrix products  24.7 us (4%)
  other arithmetic  20.4 us (3%)
  starting transfers between devices  19.1 us (3%)
  between operations  16.2 us (3%)
    all_gather x1, waiting for transfers between devices, body(): gathered = lax.all_gather(d_out, EXPERT_TENSOR, axis=0, tiled=True)  291 us
    psum x5, blocking collectives, by_axis(): return functools.reduce(lax.psum, axes, array)  74 us
    reduce_scatter x1, waiting for transfers between devices, body(): lax.psum_scatter(teacher_part.astype(jnp.bfloat16), DP_TENSOR, scatter_di...  69.8 us
    all_to_all x2, blocking collectives, sent_to_all(): return lax.all_to_all(copies, axis, split_axis=0, concat_axis=0, tiled=True)  50.8 us
    reduce_sum x3, other arithmetic, over_pieces(): return lax.all_gather(array, axis).astype(jnp.float32).sum(0)  19.8 us
    unnamed x28, local copies, waits for them, and re-layouts  15.5 us
  transfers between devices with their start and end apart: 11, of which 6 were waited for; matrix products, arithmetic and copies ran while one was open for 8% of the time, Pallas kernels for 0%

commit v1 on v0

v1 whole, which is shorter than its diff:
```python
import functools
import math

import jax
import jax.numpy as jnp
from jax import lax
from jax.experimental import pallas as pl
from jax.experimental.pallas import tpu as pltpu
from jax.sharding import Mesh
from jax.sharding import PartitionSpec as P

MESH = pl.DeviceIdType.MESH
AXES = ("dp", "x", "zl", "y", "zh")
D, ROWS, COLS, HID, SHID, TOKENS = 5120, 32, 640, 512, 128, 512
PARTS = ((0, 256, "yzx"), (256, 256, "zxy"), (512, 128, "xyz"))
GROUPS = (2, 1, 3, 0)
F32, BF16 = jnp.float32, jnp.bfloat16


def coords():
    c = {a: lax.axis_index(a) for a in AXES}
    c["z"] = c["zh"] * 2 + c["zl"]
    return c


def dev(axis, v):
    return {"zh": v // 2, "zl": v % 2} if axis == "z" else {axis: v}


def region(c, dp=None, rows=(0, ROWS), **fixed):
    at = {a: fixed.get(a, c[a]) for a in "xyz"}
    sl = {a: pl.ds(0, 4) if at[a] is None else pl.ds(at[a], 1) for a in "xy"}
    if at["z"] is None:
        zh = zl = pl.ds(0, 2)
    else:
        zh, zl = pl.ds(at["z"] // 2, 1), pl.ds(at["z"] % 2, 1)
    head = (sl["y"], zh) if dp is None else (sl["y"], zh, pl.ds(dp, 1))
    return (*head, sl["x"], zl, pl.ds(*rows))


class Links:
    def __init__(self, send_sem, recv_sem):
        self.ss, self.rs, self.n, self.started = send_sem, recv_sem, 0, []

    def number(self):
        self.n += 1
        return self.n - 1

    def copy(self, src, dst, to, k):
        return pltpu.make_async_remote_copy(
            src_ref=src, dst_ref=dst, send_sem=self.ss.at[k], recv_sem=self.rs.at[k], device_id=to, device_id_type=MESH
        )

    def send(self, src, dst, to, k):
        cp = self.copy(src, dst, to, k)
        cp.start()
        self.started.append(cp)

    def wait(self, dst, to, k):
        self.copy(dst, dst, to, k).wait_recv()

    def finish(self):
        for cp in self.started:
            cp.wait_send()


class Gather:
    def __init__(self, c, links, X, axes):
        self.c, self.ln, self.X = c, links, X
        self.a1, self.a2, self.a3 = axes
        self.k1 = [links.number() for _ in range(3)]
        self.k2 = [links.number() for _ in range(3)]
        self.k3 = [[links.number() for _ in range(4)] for _ in range(4)]
        self.kd = [links.number() for _ in range(4)]
        self.r, self.l, self.o = (c[self.a3] + 1) % 4, (c[self.a3] + 3) % 4, (c[self.a3] + 2) % 4

    def at(self, rows=(0, ROWS), dp=None, **fixed):
        return self.X.at[region(self.c, self.c["dp"] if dp is None else dp, rows, **fixed)]

    def peer(self, axis, s):
        return dev(axis, (self.c[axis] + s) % 4)

    def start1(self):
        for s in (1, 3, 2):
            self.ln.send(self.at(), self.at(), self.peer(self.a1, s), self.k1[s - 1])

    def start2(self):
        c = self.c
        for s in (1, 2, 3):
            self.ln.wait(self.at(**{self.a1: (c[self.a1] + 4 - s) % 4}), self.peer(self.a1, s), self.k1[s - 1])
        for s in (1, 3, 2):
            ref = self.at(**{self.a1: None})
            self.ln.send(ref, ref, self.peer(self.a2, s), self.k2[s - 1])
        self.ring1(0)

    def block(self, k, v3, rows=(0, ROWS)):
        return self.at(rows, **{self.a1: None, self.a2: (self.c[self.a2] + 4 - k) % 4, self.a3: v3})

    def ring1(self, k):
        if k:
            self.ln.wait(self.block(k, self.c[self.a3]), self.peer(self.a2, k), self.k2[k - 1])
        ref = self.block(k, self.c[self.a3])
        self.ln.send(ref, ref, dev(self.a3, self.r), self.k3[k][0])
        self.ln.send(ref, ref, dev(self.a3, self.l), self.k3[k][1])

    def ring2(self, k):
        self.ln.wait(self.block(k, self.l), dev(self.a3, self.r), self.k3[k][0])
        ref = self.block(k, self.l, (0, 16))
        self.ln.send(ref, ref, dev(self.a3, self.r), self.k3[k][2])
        self.ln.wait(self.block(k, self.r), dev(self.a3, self.l), self.k3[k][1])
        ref = self.block(k, self.r, (16, 16))
        self.ln.send(ref, ref, dev(self.a3, self.l), self.k3[k][3])

    def ring3(self, k):
        self.ln.wait(self.block(k, self.o, (0, 16)), dev(self.a3, self.r), self.k3[k][2])
        self.ln.wait(self.block(k, self.o, (16, 16)), dev(self.a3, self.l), self.k3[k][3])

    def plane(self, s, dp=None):
        return self.at(dp=dp, **{self.a1: None, self.a2: None, self.a3: (self.c[self.a3] + s) % 4})

    def across(self, s):
        self.ln.send(self.plane(s), self.plane(s), {"dp": 1 - self.c["dp"]}, self.kd[s])

    def crossed(self):
        for s in (0, 1, 3, 2):
            self.ln.wait(self.plane(s, 1 - self.c["dp"]), {"dp": 1 - self.c["dp"]}, self.kd[s])


def gather_rest(parts):
    for g in parts:
        g.ring2(0)
    for k in (1, 3, 2):
        for g in parts:
            g.ring1(k)
    for g in parts:
        g.across(0)
    for k in (1, 3, 2):
        for g in parts:
            g.ring2(k)
    for g in parts:
        g.across(1)
        g.across(3)
    for g in parts:
        for k in (0, 1, 3, 2):
            g.ring3(k)
        g.across(2)


class Reduce:
    def __init__(self, c, links, sums, got1, got2, got3, axes):
        self.c, self.ln, self.S, self.g1, self.g2, self.g3 = c, links, sums, got1, got2, got3
        self.a1, self.a2, self.a3 = axes
        self.k1 = [[links.number() for _ in range(6)] for _ in range(4)]
        self.k2 = [links.number() for _ in range(3)]
        self.k3 = [links.number() for _ in range(3)]
        self.r, self.l, self.o = (c[self.a3] + 1) % 4, (c[self.a3] + 3) % 4, (c[self.a3] + 2) % 4

    def idx(self, k, v3, rows=(0, ROWS)):
        v2 = (self.c[self.a2] + GROUPS[k]) % 4
        return region(self.c, None, rows, **{self.a1: None, self.a2: v2, self.a3: v3})

    def right(self, k, j, src):
        self.ln.send(src, self.g1.at[k, j], dev(self.a3, self.r), self.k1[k][j])

    def left(self, k, j, src):
        self.ln.send(src, self.g1.at[k, j], dev(self.a3, self.l), self.k1[k][j])

    def got(self, k, j):
        self.ln.wait(self.g1.at[k, j], dev(self.a3, self.r if j < 3 else self.l), self.k1[k][j])
        return self.g1[k, j].astype(F32)

    def ring1(self, k):
        S = self.S
        self.right(k, 0, S.at[self.idx(k, self.o, (0, 16))])
        self.left(k, 3, S.at[self.idx(k, self.o, (16, 16))])
        self.right(k, 1, S.at[self.idx(k, self.r, (16, 16))])
        self.left(k, 4, S.at[self.idx(k, self.l, (0, 16))])

    def ring2(self, k):
        S = self.S
        i = self.idx(k, self.r, (0, 16))
        S[i] = (S[i].astype(F32) + self.got(k, 0)).astype(BF16)
        self.right(k, 2, S.at[i])
        i = self.idx(k, self.l, (16, 16))
        S[i] = (S[i].astype(F32) + self.got(k, 3)).astype(BF16)
        self.left(k, 5, S.at[i])

    def ring3(self, k):
        S, own = self.S, self.c[self.a3]
        i = self.idx(k, own, (0, 16))
        S[i] = (S[i].astype(F32) + self.got(k, 4) + self.got(k, 2)).astype(BF16)
        i = self.idx(k, own, (16, 16))
        S[i] = (S[i].astype(F32) + self.got(k, 1) + self.got(k, 5)).astype(BF16)
        s = GROUPS[k]
        if s:
            to = dev(self.a2, (self.c[self.a2] + s) % 4)
            self.ln.send(S.at[self.idx(k, own)], self.g2.at[s - 1], to, self.k2[s - 1])

    def second(self):
        S = self.S
        i = region(self.c, **{self.a1: None})
        total = S[i].astype(F32)
        for s in (1, 2, 3):
            self.ln.wait(self.g2.at[s - 1], dev(self.a2, (self.c[self.a2] + s) % 4), self.k2[s - 1])
            total = total + self.g2[s - 1].astype(F32)
        S[i] = total.astype(BF16)
        for s in (1, 3, 2):
            v1 = (self.c[self.a1] + s) % 4
            self.ln.send(S.at[region(self.c, **{self.a1: v1})], self.g3.at[s - 1], dev(self.a1, v1), self.k3[s - 1])

    def third(self):
        total = self.S[region(self.c)].astype(F32)
        for s in (1, 2, 3):
            self.ln.wait(self.g3.at[s - 1], dev(self.a1, (self.c[self.a1] + s) % 4), self.k3[s - 1])
            total = total + self.g3[s - 1].astype(F32)
        return total


def wide(refs, y, zh):
    return jnp.concatenate([r[y, zh].reshape(TOKENS, r.shape[-1]) for r in refs], axis=1)


def kernel(tok, ids, gw, tg, tu, td, sg, su, sd, gg, gu, gd, loss, *scratch):
    X, Dx, S, R1, R2, R3 = (scratch[3 * i : 3 * i + 3] for i in range(6))
    W, WD, acc, acts, stage, sact, dcat, wt, lb, ss, rs, lsem = scratch[18:]
    c = coords()
    dp = c["dp"]
    other = {"dp": 1 - dp}
    expert = c["x"] * 2 + c["zl"]

    loads = [
        pltpu.make_async_copy(tg.at[0], W.at[:, pl.ds(0, HID)], lsem.at[0]),
        pltpu.make_async_copy(tu.at[0], W.at[:, pl.ds(HID, HID)], lsem.at[1]),
        pltpu.make_async_copy(sg, W.at[:, pl.ds(2 * HID, SHID)], lsem.at[2]),
        pltpu.make_async_copy(su, W.at[:, pl.ds(2 * HID + SHID, SHID)], lsem.at[3]),
        pltpu.make_async_copy(td.at[0], WD.at[pl.ds(dp * HID, HID)], lsem.at[4]),
        pltpu.make_async_copy(sd, WD.at[pl.ds(2 * HID, SHID)], lsem.at[5]),
    ]

    bar = pltpu.get_barrier_semaphore()
    for a in "xyz":
        for s in (1, 2, 3):
            pl.semaphore_signal(bar, inc=1, device_id=dev(a, (c[a] + s) % 4), device_id_type=MESH)
    pl.semaphore_signal(bar, inc=1, device_id=other, device_id_type=MESH)

    own = region(c, dp)
    for x, (first, width, _) in zip(X, PARTS):
        x[own] = tok[:, first : first + width][None, None, None, None, None]
    lane = lax.broadcasted_iota(jnp.int32, (ROWS, 128), 1)
    norm = gw[...] / jnp.sum(gw[...], axis=1, keepdims=True)
    weight = jnp.where(lane == ids[:, 0:1], norm[:, 0:1], 0.0) + jnp.where(lane == ids[:, 1:2], norm[:, 1:2], 0.0)
    wt[pl.ds(dp, 1), pl.ds(c["x"], 1), pl.ds(c["zl"], 1)] = weight[None, None, None]

    pl.semaphore_wait(bar, 10)
    ln = Links(ss, rs)
    parts = [Gather(c, ln, x, axes) for x, (_, _, axes) in zip(X, PARTS)]
    for g in parts:
        g.start1()
    for cp in loads:
        cp.start()

    k_td, k_h, k_zl, k_wd = (ln.number() for _ in range(4))
    k_wx = [ln.number() for _ in range(3)]
    mine = wt.at[pl.ds(dp, 1), pl.ds(c["x"], 1), pl.ds(c["zl"], 1)]
    pair = wt.at[pl.ds(dp, 1), pl.ds(c["x"], 1)]
    ln.send(mine, mine, {"zl": 1 - c["zl"]}, k_zl)
    ln.send(td.at[0], WD.at[pl.ds(dp * HID, HID)], other, k_td)
    for g in parts:
        g.start2()
    ln.wait(wt.at[pl.ds(dp, 1), pl.ds(c["x"], 1), pl.ds(1 - c["zl"], 1)], {"zl": 1 - c["zl"]}, k_zl)
    for s in (1, 2, 3):
        ln.send(pair, pair, dev("x", (c["x"] + s) % 4), k_wx[s - 1])
    gather_rest(parts)
    for s in (1, 2, 3):
        ln.wait(wt.at[pl.ds(dp, 1), pl.ds((c["x"] + 4 - s) % 4, 1)], dev("x", (c["x"] + s) % 4), k_wx[s - 1])
    ln.send(wt.at[pl.ds(dp, 1)], wt.at[pl.ds(dp, 1)], other, k_wd)
    for cp in loads:
        cp.wait()
    for g in parts:
        g.crossed()
    ln.wait(wt.at[pl.ds(1 - dp, 1)], other, k_wd)

    def up_step(i, carry):
        y, n = i // 5, i % 5
        rows = jnp.concatenate([wide(X, y, 0), wide(X, y, 1)], axis=1)
        cols = pl.ds(pl.multiple_of(n * 256, 256), 256)
        w = W[pl.ds(pl.multiple_of(y * 1280, 1280), 1280), cols]
        part = jnp.dot(rows, w, preferred_element_type=F32)

        @pl.when(y == 0)
        def _():
            acc[:, cols] = part

        @pl.when(y > 0)
        def _():
            acc[:, cols] += part

        return carry

    lax.fori_loop(0, 20, up_step, 0)

    lane = lax.broadcasted_iota(jnp.int32, (128, 128), 1)

    def act_step(i, carry):
        half = (1 - dp + i // 2) % 2
        r0 = pl.multiple_of(half * 256 + (i % 2) * 128, 128)
        rows = pl.ds(r0, 128)
        w4 = wt[half, pl.ds((i % 2) * 2, 2)].reshape(128, 128)
        w = jnp.sum(jnp.where(lane == expert, w4, 0.0), axis=1, keepdims=True)
        g, u = acc[rows, 0:HID], acc[rows, HID : 2 * HID]
        h = (g * jax.nn.sigmoid(g) * u * (-w)).astype(BF16)
        to = pl.ds(pl.multiple_of((i % 2) * 128, 128), 128)
        g, u = acc[rows, 2 * HID : 2 * HID + SHID], acc[rows, 2 * HID + SHID :]
        a = (g * jax.nn.sigmoid(g) * u).astype(BF16)
        sact[rows] = a

        @pl.when(i < 2)
        def _():
            stage[to] = h

        @pl.when(i >= 2)
        def _():
            acts[to, pl.ds(pl.multiple_of(dp * HID, HID), HID)] = h
            acts[to, 2 * HID :] = a

        return carry

    lax.fori_loop(0, 2, act_step, 0)
    there = acts.at[:, pl.ds(pl.multiple_of(dp * HID, HID), HID)]
    ln.send(stage, there, other, k_h)
    lax.fori_loop(2, 4, act_step, 0)
    ln.wait(WD.at[pl.ds((1 - dp) * HID, HID)], other, k_td)
    ln.wait(acts.at[:, pl.ds(pl.multiple_of((1 - dp) * HID, HID), HID)], other, k_h)

    reduces = [Reduce(c, ln, *refs, axes) for *refs, (_, _, axes) in zip(S, R1, R2, R3, PARTS)]
    for red, (first, width, _) in zip(reduces, PARTS):

        def down_step(t, carry):
            w = WD[:, pl.ds(pl.multiple_of(t * COLS + first, 128), width)]
            part = jnp.dot(acts[...], w, preferred_element_type=F32).astype(BF16)
            red.S[t // 2, t % 2] = part.reshape(4, 2, ROWS, width)
            return carry

        lax.fori_loop(0, 8, down_step, 0)
        for k in range(4):
            red.ring1(k)

    def turn(y, carry):
        for zh in range(2):
            for x, (first, width, _) in zip(X, PARTS):
                rows = pl.ds(pl.multiple_of(y * 1280 + zh * COLS + first, 128), width)
                W[rows, 0:TOKENS] = x[y, zh].reshape(TOKENS, width).T
        return carry

    lax.fori_loop(0, 4, turn, 0)

    for k in range(5):
        for red in reduces:
            if k < 4:
                red.ring2(k)
        for red in reduces:
            if k > 0:
                red.ring3(k - 1)
    for red in reduces:
        red.second()
    grads = [Gather(c, ln, x, axes) for x, (_, _, axes) in zip(Dx, PARTS)]
    squares = jnp.zeros((8, 128), F32)
    for red, g, (_, width, _) in zip(reduces, grads, PARTS):
        res = red.third()
        g.X[own] = (res * (1.0 / math.sqrt(TOKENS))).astype(BF16)[:, :, None]
        g.start1()
        sq = res.reshape(4, 8, width)
        sq = jnp.sum(sq * sq, axis=0)
        for j in range(width // 128):
            squares = squares + sq[:, 128 * j : 128 * j + 128]

    def loss_send(n, axis, value):
        k = [ln.number() for _ in range(3)]
        lb[n, pl.ds(c[axis], 1)] = value[None]
        count = 2 if axis == "dp" else 4
        mine = lb.at[n, pl.ds(c[axis], 1)]
        peers = [(s, (c[axis] + s) % count, (c[axis] + count - s) % count) for s in range(1, count)]
        for s, to, _ in peers:
            ln.send(mine, mine, dev(axis, to), k[s - 1])
        return n, axis, peers, k

    def loss_wait(sent):
        n, axis, peers, k = sent
        for s, to, source in peers:
            ln.wait(lb.at[n, pl.ds(source, 1)], dev(axis, to), k[s - 1])
        total = lb[n, 0] + lb[n, 1]
        return total if axis == "dp" else total + lb[n, 2] + lb[n, 3]

    sent = loss_send(0, "x", squares)
    for g in grads:
        g.start2()
    sent = loss_send(1, "y", loss_wait(sent))
    gather_rest(grads)
    sent = loss_send(2, "z", loss_wait(sent))
    sent = loss_send(3, "dp", loss_wait(sent))
    for g in grads:
        g.crossed()

    def dact_step(t, total):
        cols = pl.ds(pl.multiple_of(t * COLS, 128), COLS)
        w = WD[pl.ds(2 * HID, SHID), cols]
        d = wide(Dx, t // 2, t % 2)
        acc[:, 0:SHID] += lax.dot_general(d, w, (((1,), (1,)), ((), ())), preferred_element_type=F32)
        return total

    acc[:, 0:SHID] = jnp.zeros((TOKENS, SHID), F32)
    lax.fori_loop(0, 8, dact_step, 0)
    g, u, da = acc[:, 2 * HID : 2 * HID + SHID], acc[:, 2 * HID + SHID :], acc[:, 0:SHID]
    s = jax.nn.sigmoid(g)
    dcat[:, 0:SHID] = (da * u * s * (1.0 + g * (1.0 - s))).astype(BF16)
    dcat[:, SHID:] = (da * g * s).astype(BF16)

    def grad_step(t, carry):
        rows = pl.ds(pl.multiple_of(t * COLS, 128), COLS)
        both = jnp.dot(W[rows, 0:TOKENS], dcat[...], preferred_element_type=F32).astype(BF16)
        gg[rows] = both[:, :SHID]
        gu[rows] = both[:, SHID:]
        d = wide(Dx, t // 2, t % 2)
        gd[:, rows] = lax.dot_general(
            sact[...], d, (((0,), (0,)), ((), ())), preferred_element_type=F32
        ).astype(BF16)
        return carry

    lax.fori_loop(0, 8, grad_step, 0)
    loss[...] = jnp.full((8, 128), jnp.sum(loss_wait(sent)) / (TOKENS * D), F32)
    ln.finish()


def body(*args):
    vmem, hbm = pl.BlockSpec(memory_space=pltpu.VMEM), pl.BlockSpec(memory_space=pl.ANY)
    blocks = {"x": (1, 1, 4, 1), "y": (4, 1, 1, 1), "z": (1, 2, 1, 2)}
    whole = [pltpu.VMEM((4, 2, 2, 4, 2, ROWS, w), BF16) for _, w, _ in PARTS]
    gg, gu, gd, loss = pl.pallas_call(
        kernel,
        out_shape=(
            jax.ShapeDtypeStruct((D, SHID), BF16),
            jax.ShapeDtypeStruct((D, SHID), BF16),
            jax.ShapeDtypeStruct((SHID, D), BF16),
            jax.ShapeDtypeStruct((8, 128), F32),
        ),
        in_specs=[vmem] * 3 + [hbm] * 6,
        out_specs=(vmem,) * 4,
        scratch_shapes=[
            *whole,
            *whole,
            *[pltpu.VMEM((4, 2, 4, 2, ROWS, w), BF16) for _, w, _ in PARTS],
            *[pltpu.VMEM((4, 6, *blocks[a[0]], 16, w), BF16) for _, w, a in PARTS],
            *[pltpu.VMEM((3, *blocks[a[0]], ROWS, w), BF16) for _, w, a in PARTS],
            *[pltpu.VMEM((3, 1, 1, 1, 1, ROWS, w), BF16) for _, w, _ in PARTS],
            pltpu.VMEM((D, 2 * HID + 2 * SHID), BF16),
            pltpu.VMEM((2 * HID + SHID, D), BF16),
            pltpu.VMEM((TOKENS, 2 * HID + 2 * SHID), F32),
            pltpu.VMEM((TOKENS // 2, 2 * HID + SHID), BF16),
            pltpu.VMEM((TOKENS // 2, HID), BF16),
            pltpu.VMEM((TOKENS, SHID), BF16),
            pltpu.VMEM((TOKENS, 2 * SHID), BF16),
            pltpu.VMEM((2, 4, 2, ROWS, 128), F32),
            pltpu.VMEM((4, 4, 8, 128), F32),
            pltpu.SemaphoreType.DMA((300,)),
            pltpu.SemaphoreType.DMA((300,)),
            pltpu.SemaphoreType.DMA((6,)),
        ],
        compiler_params=pltpu.CompilerParams(
            collective_id=0, has_side_effects=True, vmem_limit_bytes=60 * 2**20
        ),
    )(*args)
    return gg, gu, gd, loss[0, 0]


def solution(mesh):
    finer = Mesh(mesh.devices.reshape(2, 4, 2, 4, 2), AXES)
    rows, tensor, expert = ("dp", "x", "zl"), ("y", "zh"), ("x", "zl")
    hidden, shards = ("dp", "y", "zh"), ("x", "zl", "y", "zh")
    return jax.shard_map(
        body,
        mesh=finer,
        in_specs=(
            P(rows, tensor),
            P(rows, None),
            P(rows, None),
            P(expert, None, hidden),
            P(expert, None, hidden),
            P(expert, hidden, None),
            P(None, shards),
            P(None, shards),
            P(shards, None),
        ),
        out_specs=(P(None, shards), P(None, shards), P(shards, None), P()),
        check_vma=False,
    )
```

time: 630 us -> 115 us (0.18)
  waiting for transfers between devices: 387 us -> 0 us
  blocking collectives: 125 us -> 0 us
  Pallas kernels: 0 us -> 104 us
  matrix products: 24.7 us -> 0 us
  local copies, waits for them, and re-layouts: 31.7 us -> 9.32 us
  other arithmetic: 20.4 us -> 0 us
  starting transfers between devices: 19.1 us -> 0 us
  between operations: 16.2 us -> 0.64 us
    all_gather x4 -> x0, waiting for transfers between devices: 291 us -> none  [the longest x1 291 us: body(): gathered = lax.all_gather(d_out, EXPERT_TENSOR, axis=0, tiled=True)]
    pallas_call x0 -> x1, Pallas kernels: none -> 104 us  [body(): pl.pallas_call(kernel, out_shape=(jax.ShapeDtypeStruct((D, SHID), BF16),...]
    psum x5 -> x0, blocking collectives: 74 us -> none  [by_axis(): return functools.reduce(lax.psum, axes, array)]
    reduce_scatter x2 -> x0, waiting for transfers between devices: 72 us -> none  [the longest x1 69.8 us: body(): lax.psum_scatter(teacher_part.astype(jnp.bfloat16), DP_TENSOR, scatter_di...]
    all_to_all x2 -> x0, blocking collectives: 50.8 us -> none  [sent_to_all(): return lax.all_to_all(copies, axis, split_axis=0, concat_axis=0, tiled=True)]
    dot_general x12 -> x0, matrix products: 24.7 us -> none  [the longest x1 4.14 us: body(): jnp.dot(shard_rows, t_gate[0], preferred_element_type=jnp.float32)]
    reduce_sum x8 -> x0, other arithmetic: 20.2 us -> none  [the longest x3 19.8 us: over_pieces(): return lax.all_gather(array, axis).astype(jnp.float32).sum(0)]
    all_to_all x4 -> x0, starting transfers between devices: 18.7 us -> none  [the longest x1 7.26 us: sent_to_all(): return lax.all_to_all(copies, axis, split_axis=0, concat_axis=0, tiled=True)]
  transfers between devices with their start and end apart: 11 -> 0, of which waited for: 6 -> 0; matrix products, arithmetic and copies ran while one was open for 8% -> 0% of each run, Pallas kernels for 0% -> 0%
where the time goes in v1:
time: 115 us; the launch traced here: 114 us
  Pallas kernels  104 us (90%)
  local copies, waits for them, and re-layouts  9.32 us (8%)
    pallas_call x1, Pallas kernels, body(): pl.pallas_call(kernel, out_shape=(jax.ShapeDtypeStruct((D, SHID), BF16),...  104 us
    unnamed x9, local copies, waits for them, and re-layouts  8.14 us

profile of v1, /device:TPU:1, one launch (start us, length us, event | category | flops | bytes accessed | tf_op | source)
XLA Modules:
  0.0 114.0 jit_solution(17316452079659278357)
XLA Ops:
  0.6 1.4 %copy.13.ids = s32[32,2]{1,0:T(8,128)} copy(s32[32,2]{0,1:T(2,128)} %param.10) | data formatting | bytes 512 | tf_op args[1]
  2.0 1.4 %copy.14.gw = f32[32,2]{1,0:T(8,128)} copy(f32[32,2]{0,1:T(2,128)} %param.11) | data formatting | bytes 512 | tf_op args[2]
  3.4 104.0 %shard_map.120 = (bf16[5120,128]{1,0:T(8,128)(2,1)}, bf16[5120,128]{1,0:T(8,128)(2,1)}, bf16[128,5120]{1,0:T(8,128)(2,1)}, f32[8,128]{1,0:T(8,128)}) custom-call(bf16[32,640]{1,0:T(8,128)(2,1)} %tok.1, s32[32,2]{1,0:T(8,128)} %copy.13.ids, f32[32,2]{1,0:T(8,128)} %copy.14.gw, bf16[1,5120,512]{2,1,0:T(8,128)(2,1)} %tg.1, bf16[1,5120,512]{2,1,0:T(8,128)(2,1)} %tu.1, ...), custom_call_target="tpu_custom_call" | custom-call | tf_op jit(solution)/shard_map/pallas_call | solution.py:438
  107.4 1.2 %slice.3 = f32[1,1]{1,0:T(1,128)} slice(f32[8,128]{1,0:T(8,128)} %get-tuple-element.11), slice={[0:1], [0:1]} | slice | bytes 8 | tf_op jit(solution)/shard_map/slice | solution.py:472
  108.6 0.0 copy-start.1
  108.6 2.6 %copy.18 = bf16[5120,128]{1,0:T(8,128)(2,1)} copy(bf16[5120,128]{1,0:T(8,128)(2,1)} %get-tuple-element.16) | data formatting | bytes 2621440
  111.2 0.0 copy-done.1
  111.2 0.0 copy-start
  111.2 1.1 copy.19
  112.2 0.7 copy-done
  113.0 1.1 copy.20
Async XLA Ops:
  108.6 2.6 %copy-start.1 = (bf16[5120,128]{1,0:T(8,128)(2,1)S(1)}, bf16[5120,128]{1,0:T(8,128)(2,1)}, u32[]{:S(2)}) copy-start(bf16[5120,128]{1,0:T(8,128)(2,1)} %get-tuple-element.17) | copy-start | bytes 3932164
  111.2 1.8 %copy-start = (bf16[128,5120]{1,0:T(8,128)(2,1)S(1)}, bf16[128,5120]{1,0:T(8,128)(2,1)}, u32[]{:S(2)}) copy-start(bf16[128,5120]{1,0:T(8,128)(2,1)} %get-tuple-element.18) | copy-start | bytes 3932164

commit v2 on v1

--- a/solution.py
+++ b/solution.py
@@ -72,6 +72,7 @@
         self.k2 = [links.number() for _ in range(3)]
         self.k3 = [[links.number() for _ in range(4)] for _ in range(4)]
         self.kd = [links.number() for _ in range(4)]
+        self.ko = [links.number() for _ in range(4)]
         self.r, self.l, self.o = (c[self.a3] + 1) % 4, (c[self.a3] + 3) % 4, (c[self.a3] + 2) % 4
 
     def at(self, rows=(0, ROWS), dp=None, **fixed):
@@ -114,6 +115,8 @@
     def ring3(self, k):
         self.ln.wait(self.block(k, self.o, (0, 16)), dev(self.a3, self.r), self.k3[k][2])
         self.ln.wait(self.block(k, self.o, (16, 16)), dev(self.a3, self.l), self.k3[k][3])
+        ref = self.block(k, self.o)
+        self.ln.send(ref, ref, {"dp": 1 - self.c["dp"]}, self.ko[k])
 
     def plane(self, s, dp=None):
         return self.at(dp=dp, **{self.a1: None, self.a2: None, self.a3: (self.c[self.a3] + s) % 4})
@@ -121,12 +124,18 @@
     def across(self, s):
         self.ln.send(self.plane(s), self.plane(s), {"dp": 1 - self.c["dp"]}, self.kd[s])
 
-    def crossed(self):
-        for s in (0, 1, 3, 2):
-            self.ln.wait(self.plane(s, 1 - self.c["dp"]), {"dp": 1 - self.c["dp"]}, self.kd[s])
-
-
-def gather_rest(parts):
+    def crossed(self, s):
+        dp = 1 - self.c["dp"]
+        if s == 2:
+            for k in (0, 1, 3, 2):
+                at = {self.a1: None, self.a2: (self.c[self.a2] + 4 - k) % 4, self.a3: self.o}
+                self.ln.wait(self.at(dp=dp, **at), {"dp": dp}, self.ko[k])
+        else:
+            self.ln.wait(self.plane(s, dp), {"dp": dp}, self.kd[s])
+        return (self.c[self.a3] + s) % 4
+
+
+def gather_rest(parts, use):
     for g in parts:
         g.ring2(0)
     for k in (1, 3, 2):
@@ -134,16 +143,25 @@
             g.ring1(k)
     for g in parts:
         g.across(0)
-    for k in (1, 3, 2):
-        for g in parts:
-            g.ring2(k)
-    for g in parts:
+    for i in (0, 1):
+        use(i, parts[i].crossed(0))
+    for g in parts:
+        g.ring2(1)
+    use(2, parts[2].crossed(0))
+    for g in parts:
+        g.ring2(3)
+    for g in parts:
+        g.ring2(2)
         g.across(1)
         g.across(3)
-    for g in parts:
-        for k in (0, 1, 3, 2):
+    for i, g in enumerate(parts):
+        use(i, g.crossed(1))
+    for k in (0, 1, 3, 2):
+        for g in parts:
             g.ring3(k)
-        g.across(2)
+    for s in (3, 2):
+        for i, g in enumerate(parts):
+            use(i, g.crossed(s))
 
 
 class Reduce:
@@ -220,14 +238,46 @@
     return jnp.concatenate([r[y, zh].reshape(TOKENS, r.shape[-1]) for r in refs], axis=1)
 
 
-def kernel(tok, ids, gw, tg, tu, td, sg, su, sd, gg, gu, gd, loss, *scratch):
+def add_plane(total, x, v, axis, first, width, w, flipped):
+    if axis == "x":
+        tiles = [x[t // 2, t % 2, :, pl.ds(v, 1)].reshape(128, width) for t in range(8)]
+        starts = [t * COLS + first for t in range(8)]
+    elif axis == "y":
+        tiles = [x[v, zh].reshape(TOKENS, width) for zh in range(2)]
+        starts = [pl.multiple_of((v * 2 + zh) * COLS + first, 128) for zh in range(2)]
+    else:
+        tiles = [x[y, v // 2, :, :, pl.ds(v % 2, 1)].reshape(256, width) for y in range(4)]
+        starts = [pl.multiple_of((y * 2 + v // 2) * COLS + first, 128) for y in range(4)]
+    lhs = jnp.concatenate(tiles, axis=1)
+    if flipped:
+        rhs = jnp.concatenate([w[pl.ds(2 * HID, SHID), pl.ds(a, width)] for a in starts], axis=1)
+        part = lax.dot_general(lhs, rhs, (((1,), (1,)), ((), ())), preferred_element_type=F32)
+    else:
+        rhs = jnp.concatenate([w[pl.ds(a, width)] for a in starts], axis=0)
+        part = jnp.dot(lhs, rhs, preferred_element_type=F32)
+    n = part.shape[-1]
+    if axis == "x":
+        total[:, pl.ds(v, 1)] += part.reshape(2, 1, 2, ROWS, n)
+    elif axis == "y":
+        total[...] += part.reshape(2, 4, 2, ROWS, n)
+    else:
+        total[:, :, pl.ds(v % 2, 1)] += part.reshape(2, 4, 1, ROWS, n)
+
+
+def kernel(tok, ids_in, gw_in, tg, tu, td, sg, su, sd, gg, gu, gd, loss, *scratch):
     X, Dx, S, R1, R2, R3 = (scratch[3 * i : 3 * i + 3] for i in range(6))
-    W, WD, acc, acts, stage, sact, dcat, wt, lb, ss, rs, lsem = scratch[18:]
+    ids, gw, W, WD, acc, dacc, acts, stage, sact, dcat, wt, turned, lb, ss, rs, lsem = scratch[18:]
     c = coords()
     dp = c["dp"]
     other = {"dp": 1 - dp}
     expert = c["x"] * 2 + c["zl"]
 
+    first_loads = [
+        pltpu.make_async_copy(tok.at[:, pl.ds(first, width)], x.at[c["y"], c["zh"], dp, c["x"], c["zl"]], lsem.at[6 + n])
+        for n, (x, (first, width, _)) in enumerate(zip(X, PARTS))
+    ]
+    first_loads.append(pltpu.make_async_copy(ids_in, ids, lsem.at[9]))
+    first_loads.append(pltpu.make_async_copy(gw_in, gw, lsem.at[10]))
     loads = [
         pltpu.make_async_copy(tg.at[0], W.at[:, pl.ds(0, HID)], lsem.at[0]),
         pltpu.make_async_copy(tu.at[0], W.at[:, pl.ds(HID, HID)], lsem.at[1]),
@@ -237,6 +287,8 @@
         pltpu.make_async_copy(sd, WD.at[pl.ds(2 * HID, SHID)], lsem.at[5]),
     ]
 
+    for cp in first_loads + loads:
+        cp.start()
     bar = pltpu.get_barrier_semaphore()
     for a in "xyz":
         for s in (1, 2, 3):
@@ -244,11 +296,14 @@
     pl.semaphore_signal(bar, inc=1, device_id=other, device_id_type=MESH)
 
     own = region(c, dp)
-    for x, (first, width, _) in zip(X, PARTS):
-        x[own] = tok[:, first : first + width][None, None, None, None, None]
-    lane = lax.broadcasted_iota(jnp.int32, (ROWS, 128), 1)
-    norm = gw[...] / jnp.sum(gw[...], axis=1, keepdims=True)
-    weight = jnp.where(lane == ids[:, 0:1], norm[:, 0:1], 0.0) + jnp.where(lane == ids[:, 1:2], norm[:, 1:2], 0.0)
+    acc[...] = jnp.zeros_like(acc)
+    for cp in first_loads:
+        cp.wait()
+    norm = gw[...] / jnp.sum(gw[...], axis=0, keepdims=True)
+    sub = lax.broadcasted_iota(jnp.int32, (8, ROWS), 0)
+    turned[...] = jnp.zeros_like(turned)
+    turned[0:8, 0:ROWS] = jnp.where(sub == ids[0:1], norm[0:1], 0.0) + jnp.where(sub == ids[1:2], norm[1:2], 0.0)
+    weight = turned[...].T[0:ROWS]
     wt[pl.ds(dp, 1), pl.ds(c["x"], 1), pl.ds(c["zl"], 1)] = weight[None, None, None]
 
     pl.semaphore_wait(bar, 10)
@@ -256,8 +311,6 @@
     parts = [Gather(c, ln, x, axes) for x, (_, _, axes) in zip(X, PARTS)]
     for g in parts:
         g.start1()
-    for cp in loads:
-        cp.start()
 
     k_td, k_h, k_zl, k_wd = (ln.number() for _ in range(4))
     k_wx = [ln.number() for _ in range(3)]
@@ -270,49 +323,36 @@
     ln.wait(wt.at[pl.ds(dp, 1), pl.ds(c["x"], 1), pl.ds(1 - c["zl"], 1)], {"zl": 1 - c["zl"]}, k_zl)
     for s in (1, 2, 3):
         ln.send(pair, pair, dev("x", (c["x"] + s) % 4), k_wx[s - 1])
-    gather_rest(parts)
+
+    def up(i, v):
+        while loads:
+            loads.pop().wait()
+        first, width, axes = PARTS[i]
+        add_plane(acc, X[i], v, axes[2], first, width, W, False)
+
+    gather_rest(parts, up)
     for s in (1, 2, 3):
         ln.wait(wt.at[pl.ds(dp, 1), pl.ds((c["x"] + 4 - s) % 4, 1)], dev("x", (c["x"] + s) % 4), k_wx[s - 1])
     ln.send(wt.at[pl.ds(dp, 1)], wt.at[pl.ds(dp, 1)], other, k_wd)
-    for cp in loads:
-        cp.wait()
-    for g in parts:
-        g.crossed()
     ln.wait(wt.at[pl.ds(1 - dp, 1)], other, k_wd)
-
-    def up_step(i, carry):
-        y, n = i // 5, i % 5
-        rows = jnp.concatenate([wide(X, y, 0), wide(X, y, 1)], axis=1)
-        cols = pl.ds(pl.multiple_of(n * 256, 256), 256)
-        w = W[pl.ds(pl.multiple_of(y * 1280, 1280), 1280), cols]
-        part = jnp.dot(rows, w, preferred_element_type=F32)
-
-        @pl.when(y == 0)
-        def _():
-            acc[:, cols] = part
-
-        @pl.when(y > 0)
-        def _():
-            acc[:, cols] += part
-
-        return carry
-
-    lax.fori_loop(0, 20, up_step, 0)
 
     lane = lax.broadcasted_iota(jnp.int32, (128, 128), 1)
 
     def act_step(i, carry):
         half = (1 - dp + i // 2) % 2
-        r0 = pl.multiple_of(half * 256 + (i % 2) * 128, 128)
-        rows = pl.ds(r0, 128)
-        w4 = wt[half, pl.ds((i % 2) * 2, 2)].reshape(128, 128)
+        two = pl.ds((i % 2) * 2, 2)
+        w4 = wt[half, two].reshape(128, 128)
         w = jnp.sum(jnp.where(lane == expert, w4, 0.0), axis=1, keepdims=True)
-        g, u = acc[rows, 0:HID], acc[rows, HID : 2 * HID]
+
+        def cols(a, n):
+            return acc[half, two, :, :, a : a + n].reshape(128, n)
+
+        g, u = cols(0, HID), cols(HID, HID)
         h = (g * jax.nn.sigmoid(g) * u * (-w)).astype(BF16)
         to = pl.ds(pl.multiple_of((i % 2) * 128, 128), 128)
-        g, u = acc[rows, 2 * HID : 2 * HID + SHID], acc[rows, 2 * HID + SHID :]
+        g, u = cols(2 * HID, SHID), cols(2 * HID + SHID, SHID)
         a = (g * jax.nn.sigmoid(g) * u).astype(BF16)
-        sact[rows] = a
+        sact[pl.ds(pl.multiple_of(half * 256 + (i % 2) * 128, 128), 128)] = a
 
         @pl.when(i < 2)
         def _():
@@ -333,17 +373,16 @@
     ln.wait(acts.at[:, pl.ds(pl.multiple_of((1 - dp) * HID, HID), HID)], other, k_h)
 
     reduces = [Reduce(c, ln, *refs, axes) for *refs, (_, _, axes) in zip(S, R1, R2, R3, PARTS)]
-    for red, (first, width, _) in zip(reduces, PARTS):
-
-        def down_step(t, carry):
-            w = WD[:, pl.ds(pl.multiple_of(t * COLS + first, 128), width)]
+    for n, (red, (first, width, _)) in enumerate(zip(reduces, PARTS)):
+        for y in (0, 2):
+            w = jnp.concatenate([WD[:, (2 * y + t) * COLS + first : (2 * y + t) * COLS + first + width] for t in range(4)], axis=1)
             part = jnp.dot(acts[...], w, preferred_element_type=F32).astype(BF16)
-            red.S[t // 2, t % 2] = part.reshape(4, 2, ROWS, width)
-            return carry
-
-        lax.fori_loop(0, 8, down_step, 0)
+            for t in range(4):
+                red.S[y + t // 2, t % 2] = part[:, t * width : (t + 1) * width].reshape(4, 2, ROWS, width)
         for k in range(4):
             red.ring1(k)
+        if n == 1:
+            reduces[0].ring2(0)
 
     def turn(y, carry):
         for zh in range(2):
@@ -356,7 +395,7 @@
 
     for k in range(5):
         for red in reduces:
-            if k < 4:
+            if k < 4 and not (k == 0 and red is reduces[0]):
                 red.ring2(k)
         for red in reduces:
             if k > 0:
@@ -395,22 +434,24 @@
     for g in grads:
         g.start2()
     sent = loss_send(1, "y", loss_wait(sent))
-    gather_rest(grads)
-    sent = loss_send(2, "z", loss_wait(sent))
-    sent = loss_send(3, "dp", loss_wait(sent))
-    for g in grads:
-        g.crossed()
-
-    def dact_step(t, total):
-        cols = pl.ds(pl.multiple_of(t * COLS, 128), COLS)
-        w = WD[pl.ds(2 * HID, SHID), cols]
-        d = wide(Dx, t // 2, t % 2)
-        acc[:, 0:SHID] += lax.dot_general(d, w, (((1,), (1,)), ((), ())), preferred_element_type=F32)
-        return total
-
-    acc[:, 0:SHID] = jnp.zeros((TOKENS, SHID), F32)
-    lax.fori_loop(0, 8, dact_step, 0)
-    g, u, da = acc[:, 2 * HID : 2 * HID + SHID], acc[:, 2 * HID + SHID :], acc[:, 0:SHID]
+
+    stages = []
+
+    def back(i, v):
+        nonlocal sent
+        first, width, axes = PARTS[i]
+        if len(stages) == 0:
+            sent = loss_send(2, "z", loss_wait(sent))
+        if len(stages) == 3:
+            sent = loss_send(3, "dp", loss_wait(sent))
+        stages.append(i)
+        add_plane(dacc, Dx[i], v, axes[2], first, width, WD, True)
+
+    dacc[...] = jnp.zeros_like(dacc)
+    gather_rest(grads, back)
+
+    g, u = (acc[..., a : a + SHID].reshape(TOKENS, SHID) for a in (2 * HID, 2 * HID + SHID))
+    da = dacc[...].reshape(TOKENS, SHID)
     s = jax.nn.sigmoid(g)
     dcat[:, 0:SHID] = (da * u * s * (1.0 + g * (1.0 - s))).astype(BF16)
     dcat[:, SHID:] = (da * g * s).astype(BF16)
@@ -427,12 +468,20 @@
         return carry
 
     lax.fori_loop(0, 8, grad_step, 0)
-    loss[...] = jnp.full((8, 128), jnp.sum(loss_wait(sent)) / (TOKENS * D), F32)
+    loss[...] = jnp.sum(loss_wait(sent), keepdims=True) / (TOKENS * D)
     ln.finish()
 
 
+def placed(a, b, c, a_out, b_out, c_out, sems):
+    copies = [pltpu.make_async_copy(*refs, sems.at[n]) for n, refs in enumerate(((a, a_out), (b, b_out), (c, c_out)))]
+    for cp in copies:
+        cp.start()
+    for cp in copies:
+        cp.wait()
+
+
 def body(*args):
-    vmem, hbm = pl.BlockSpec(memory_space=pltpu.VMEM), pl.BlockSpec(memory_space=pl.ANY)
+    vmem, hbm = pl.BlockSpec(memory_space=pltpu.VMEM), pl.BlockSpec(memory_space=pltpu.HBM)
     blocks = {"x": (1, 1, 4, 1), "y": (4, 1, 1, 1), "z": (1, 2, 1, 2)}
     whole = [pltpu.VMEM((4, 2, 2, 4, 2, ROWS, w), BF16) for _, w, _ in PARTS]
     gg, gu, gd, loss = pl.pallas_call(
@@ -441,9 +490,9 @@
             jax.ShapeDtypeStruct((D, SHID), BF16),
             jax.ShapeDtypeStruct((D, SHID), BF16),
             jax.ShapeDtypeStruct((SHID, D), BF16),
-            jax.ShapeDtypeStruct((8, 128), F32),
+            jax.ShapeDtypeStruct((1, 1), F32),
         ),
-        in_specs=[vmem] * 3 + [hbm] * 6,
+        in_specs=[hbm] * 9,
         out_specs=(vmem,) * 4,
         scratch_shapes=[
             *whole,
@@ -452,23 +501,36 @@
             *[pltpu.VMEM((4, 6, *blocks[a[0]], 16, w), BF16) for _, w, a in PARTS],
             *[pltpu.VMEM((3, *blocks[a[0]], ROWS, w), BF16) for _, w, a in PARTS],
             *[pltpu.VMEM((3, 1, 1, 1, 1, ROWS, w), BF16) for _, w, _ in PARTS],
+            pltpu.VMEM((2, ROWS), jnp.int32),
+            pltpu.VMEM((2, ROWS), F32),
             pltpu.VMEM((D, 2 * HID + 2 * SHID), BF16),
             pltpu.VMEM((2 * HID + SHID, D), BF16),
-            pltpu.VMEM((TOKENS, 2 * HID + 2 * SHID), F32),
+            pltpu.VMEM((2, 4, 2, ROWS, 2 * HID + 2 * SHID), F32),
+            pltpu.VMEM((2, 4, 2, ROWS, SHID), F32),
             pltpu.VMEM((TOKENS // 2, 2 * HID + SHID), BF16),
             pltpu.VMEM((TOKENS // 2, HID), BF16),
             pltpu.VMEM((TOKENS, SHID), BF16),
             pltpu.VMEM((TOKENS, 2 * SHID), BF16),
             pltpu.VMEM((2, 4, 2, ROWS, 128), F32),
+            pltpu.VMEM((128, 128), F32),
             pltpu.VMEM((4, 4, 8, 128), F32),
             pltpu.SemaphoreType.DMA((300,)),
             pltpu.SemaphoreType.DMA((300,)),
-            pltpu.SemaphoreType.DMA((6,)),
+            pltpu.SemaphoreType.DMA((11,)),
         ],
         compiler_params=pltpu.CompilerParams(
-            collective_id=0, has_side_effects=True, vmem_limit_bytes=60 * 2**20
+            collective_id=0, has_side_effects=True, vmem_limit_bytes=50 * 2**20
         ),
-    )(*args)
+    )(args[0], args[1].T, args[2].T, *args[3:])
+    anywhere = pl.BlockSpec(memory_space=pl.ANY)
+    gg, gu, gd = pl.pallas_call(
+        placed,
+        out_shape=tuple(jax.ShapeDtypeStruct(a.shape, BF16) for a in (gg, gu, gd)),
+        in_specs=[anywhere] * 3,
+        out_specs=(pl.BlockSpec(memory_space=pltpu.HBM),) * 3,
+        scratch_shapes=[pltpu.SemaphoreType.DMA((3,))],
+        compiler_params=pltpu.CompilerParams(vmem_limit_bytes=4 * 2**20),
+    )(gg, gu, gd)
     return gg, gu, gd, loss[0, 0]
 
 

time: 115 us -> 96.1 us (0.84)
  Pallas kernels: 104 us -> 91.4 us
  local copies, waits for them, and re-layouts: 9.32 us -> 2.13 us
  between operations: 0.64 us -> 2.4 us
    pallas_call x1, Pallas kernels: 104 us -> 89.4 us  [body(): pl.pallas_call(kernel, out_shape=(jax.ShapeDtypeStruct((D, SHID), BF16),...]
    unnamed x9 -> x6, local copies, waits for them, and re-layouts: 8.14 us -> 2.13 us
    pallas_call x0 -> x1, Pallas kernels: none -> 1.95 us  [body(): pl.pallas_call(placed, out_shape=tuple((jax.ShapeDtypeStruct(a.shape, BF1...]
    slice x1 -> x0, local copies, waits for them, and re-layouts: 1.19 us -> none  [body(): return (gg, gu, gd, loss[0, 0])]
where the time goes in v2:
time: 96.1 us; the launch traced here: 95.9 us
  Pallas kernels  91.4 us (95%)
  between operations  2.4 us (2%)
  local copies, waits for them, and re-layouts  2.13 us (2%)
    pallas_call x1, Pallas kernels, body(): pl.pallas_call(kernel, out_shape=(jax.ShapeDtypeStruct((D, SHID), BF16),...  89.4 us
    unnamed x6, local copies, waits for them, and re-layouts  2.13 us
    pallas_call x1, Pallas kernels, body(): pl.pallas_call(placed, out_shape=tuple((jax.ShapeDtypeStruct(a.shape, BF1...  1.95 us

profile of v2, /device:TPU:1, one launch (start us, length us, event | category | flops | bytes accessed | tf_op | source)
XLA Modules:
  0.0 95.9 jit_solution(6195386088153817392)
XLA Ops:
  0.6 0.0 copy-start
  0.6 0.8 copy-done
  1.4 0.0 copy-start.1
  1.4 0.7 copy-done.1
  2.1 0.0 copy-start.2
  2.1 0.7 copy-done.2
  2.8 89.4 %shard_map.120 = (bf16[5120,128]{1,0:T(8,128)(2,1)S(1)}, bf16[5120,128]{1,0:T(8,128)(2,1)S(1)}, bf16[128,5120]{1,0:T(8,128)(2,1)S(1)}, f32[1,1]{1,0:T(1,128)}) custom-call(bf16[32,640]{1,0:T(8,128)(2,1)S(1)} %copy-done, s32[2,32]{1,0:T(2,128)S(1)} %bitcast.3, f32[2,32]{1,0:T(2,128)S(1)} %bitcast.4, bf16[1,5120,512]{2,1,0:T(8,128)(2,1)} %tg.1, ...), custom_call_target="tpu_custom_call" | custom-call | tf_op jit(solution)/shard_map/pallas_call | solution.py:487
  92.2 1.9 %shard_map.121 = (bf16[5120,128]{1,0:T(8,128)(2,1)}, bf16[5120,128]{1,0:T(8,128)(2,1)}, bf16[128,5120]{1,0:T(8,128)(2,1)}) custom-call(bf16[5120,128]{1,0:T(8,128)(2,1)S(1)} %get-tuple-element.11.a, bf16[5120,128]{1,0:T(8,128)(2,1)S(1)} %get-tuple-element.12.b, bf16[128,5120]{1,0:T(8,128)(2,1)S(1)} %get-tuple-element.13.c), custom_call_target="tpu_custom_call" | custom-call | tf_op jit(solution)/shard_map/pallas_call | solution.py:526
Async XLA Ops:
  0.6 0.8 copy-start
  1.4 0.7 copy-start.1
  2.1 0.7 copy-start.2

commit v3 on v2

--- a/solution.py
+++ b/solution.py
@@ -13,7 +13,8 @@
 AXES = ("dp", "x", "zl", "y", "zh")
 D, ROWS, COLS, HID, SHID, TOKENS = 5120, 32, 640, 512, 128, 512
 PARTS = ((0, 256, "yzx"), (256, 256, "zxy"), (512, 128, "xyz"))
-GROUPS = (2, 1, 3, 0)
+GROUPS = (2, 3, 1, 0)
+RECEIVES = 241
 F32, BF16 = jnp.float32, jnp.bfloat16
 
 
@@ -39,8 +40,9 @@
 
 
 class Links:
-    def __init__(self, send_sem, recv_sem):
-        self.ss, self.rs, self.n, self.started = send_sem, recv_sem, 0, []
+    def __init__(self, send_sem, recv_sem, filler):
+        self.ss, self.rs, self.n = send_sem, recv_sem, 0
+        self.filler, self.batch, self.tiles = filler, 0, 0
 
     def number(self):
         self.n += 1
@@ -48,20 +50,32 @@
 
     def copy(self, src, dst, to, k):
         return pltpu.make_async_remote_copy(
-            src_ref=src, dst_ref=dst, send_sem=self.ss.at[k], recv_sem=self.rs.at[k], device_id=to, device_id_type=MESH
+            src_ref=src,
+            dst_ref=dst,
+            send_sem=self.ss.at[self.batch],
+            recv_sem=self.rs.at[k],
+            device_id=to,
+            device_id_type=MESH,
         )
 
     def send(self, src, dst, to, k):
-        cp = self.copy(src, dst, to, k)
-        cp.start()
-        self.started.append(cp)
+        self.copy(src, dst, to, k).start()
+        self.tiles += math.prod(src.shape) * jnp.dtype(src.dtype).itemsize // 4096
 
     def wait(self, dst, to, k):
         self.copy(dst, dst, to, k).wait_recv()
 
-    def finish(self):
-        for cp in self.started:
-            cp.wait_send()
+    def taken(self):
+        batch = self.batch, self.tiles
+        self.batch, self.tiles = self.batch + 1, 0
+        return batch
+
+    def finish(self, batch):
+        n, tiles = batch
+        wide = max(b for b in range(1, 11) if tiles % b == 0)
+        assert tiles // wide <= 320
+        ref = self.filler.at[pl.ds(0, tiles // wide * 16), pl.ds(0, wide * 128)]
+        pltpu.make_async_copy(ref, ref, self.ss.at[n]).wait()
 
 
 class Gather:
@@ -70,9 +84,8 @@
         self.a1, self.a2, self.a3 = axes
         self.k1 = [links.number() for _ in range(3)]
         self.k2 = [links.number() for _ in range(3)]
-        self.k3 = [[links.number() for _ in range(4)] for _ in range(4)]
+        self.k3 = [[links.number() for _ in range(3)] for _ in range(4)]
         self.kd = [links.number() for _ in range(4)]
-        self.ko = [links.number() for _ in range(4)]
         self.r, self.l, self.o = (c[self.a3] + 1) % 4, (c[self.a3] + 3) % 4, (c[self.a3] + 2) % 4
 
     def at(self, rows=(0, ROWS), dp=None, **fixed):
@@ -110,13 +123,12 @@
         self.ln.send(ref, ref, dev(self.a3, self.r), self.k3[k][2])
         self.ln.wait(self.block(k, self.r), dev(self.a3, self.l), self.k3[k][1])
         ref = self.block(k, self.r, (16, 16))
-        self.ln.send(ref, ref, dev(self.a3, self.l), self.k3[k][3])
+        self.ln.send(ref, ref, dev(self.a3, self.l), self.k3[k][2])
 
     def ring3(self, k):
-        self.ln.wait(self.block(k, self.o, (0, 16)), dev(self.a3, self.r), self.k3[k][2])
-        self.ln.wait(self.block(k, self.o, (16, 16)), dev(self.a3, self.l), self.k3[k][3])
         ref = self.block(k, self.o)
-        self.ln.send(ref, ref, {"dp": 1 - self.c["dp"]}, self.ko[k])
+        self.ln.wait(ref, dev(self.a3, self.r), self.k3[k][2])
+        self.ln.send(ref, ref, {"dp": 1 - self.c["dp"]}, self.kd[2])
 
     def plane(self, s, dp=None):
         return self.at(dp=dp, **{self.a1: None, self.a2: None, self.a3: (self.c[self.a3] + s) % 4})
@@ -126,12 +138,7 @@
 
     def crossed(self, s):
         dp = 1 - self.c["dp"]
-        if s == 2:
-            for k in (0, 1, 3, 2):
-                at = {self.a1: None, self.a2: (self.c[self.a2] + 4 - k) % 4, self.a3: self.o}
-                self.ln.wait(self.at(dp=dp, **at), {"dp": dp}, self.ko[k])
-        else:
-            self.ln.wait(self.plane(s, dp), {"dp": dp}, self.kd[s])
+        self.ln.wait(self.plane(s, dp), {"dp": dp}, self.kd[s])
         return (self.c[self.a3] + s) % 4
 
 
@@ -174,7 +181,7 @@
         self.r, self.l, self.o = (c[self.a3] + 1) % 4, (c[self.a3] + 3) % 4, (c[self.a3] + 2) % 4
 
     def idx(self, k, v3, rows=(0, ROWS)):
-        v2 = (self.c[self.a2] + GROUPS[k]) % 4
+        v2 = self.c[self.a2] ^ GROUPS[k]
         return region(self.c, None, rows, **{self.a1: None, self.a2: v2, self.a3: v3})
 
     def right(self, k, j, src):
@@ -211,7 +218,7 @@
         S[i] = (S[i].astype(F32) + self.got(k, 1) + self.got(k, 5)).astype(BF16)
         s = GROUPS[k]
         if s:
-            to = dev(self.a2, (self.c[self.a2] + s) % 4)
+            to = dev(self.a2, self.c[self.a2] ^ s)
             self.ln.send(S.at[self.idx(k, own)], self.g2.at[s - 1], to, self.k2[s - 1])
 
     def second(self):
@@ -219,7 +226,7 @@
         i = region(self.c, **{self.a1: None})
         total = S[i].astype(F32)
         for s in (1, 2, 3):
-            self.ln.wait(self.g2.at[s - 1], dev(self.a2, (self.c[self.a2] + s) % 4), self.k2[s - 1])
+            self.ln.wait(self.g2.at[s - 1], dev(self.a2, self.c[self.a2] ^ s), self.k2[s - 1])
             total = total + self.g2[s - 1].astype(F32)
         S[i] = total.astype(BF16)
         for s in (1, 3, 2):
@@ -307,7 +314,7 @@
     wt[pl.ds(dp, 1), pl.ds(c["x"], 1), pl.ds(c["zl"], 1)] = weight[None, None, None]
 
     pl.semaphore_wait(bar, 10)
-    ln = Links(ss, rs)
+    ln = Links(ss, rs, W)
     parts = [Gather(c, ln, x, axes) for x, (_, _, axes) in zip(X, PARTS)]
     for g in parts:
         g.start1()
@@ -367,20 +374,33 @@
 
     lax.fori_loop(0, 2, act_step, 0)
     there = acts.at[:, pl.ds(pl.multiple_of(dp * HID, HID), HID)]
+    gathered = ln.taken()
     ln.send(stage, there, other, k_h)
+    staged = ln.taken()
     lax.fori_loop(2, 4, act_step, 0)
     ln.wait(WD.at[pl.ds((1 - dp) * HID, HID)], other, k_td)
     ln.wait(acts.at[:, pl.ds(pl.multiple_of((1 - dp) * HID, HID), HID)], other, k_h)
 
     reduces = [Reduce(c, ln, *refs, axes) for *refs, (_, _, axes) in zip(S, R1, R2, R3, PARTS)]
     for n, (red, (first, width, _)) in enumerate(zip(reduces, PARTS)):
-        for y in (0, 2):
-            w = jnp.concatenate([WD[:, (2 * y + t) * COLS + first : (2 * y + t) * COLS + first + width] for t in range(4)], axis=1)
+        for half in (0, 1):
+            if n == 0:
+                zh = (c["zh"] + 1 + half) % 2
+                shards = [(y, zh) for y in range(4)]
+            else:
+                shards = [(2 * half + t // 2, t % 2) for t in range(4)]
+            w = jnp.concatenate(
+                [WD[:, pl.ds(pl.multiple_of((y * 2 + zh) * COLS + first, 128), width)] for y, zh in shards], axis=1
+            )
             part = jnp.dot(acts[...], w, preferred_element_type=F32).astype(BF16)
-            for t in range(4):
-                red.S[y + t // 2, t % 2] = part[:, t * width : (t + 1) * width].reshape(4, 2, ROWS, width)
-        for k in range(4):
-            red.ring1(k)
+            for t, (y, zh) in enumerate(shards):
+                red.S[y, zh] = part[:, t * width : (t + 1) * width].reshape(4, 2, ROWS, width)
+            if n == 0:
+                red.ring1(2 * half)
+                red.ring1(2 * half + 1)
+        if n > 0:
+            for k in range(4):
+                red.ring1(k)
         if n == 1:
             reduces[0].ring2(0)
 
@@ -392,6 +412,8 @@
         return carry
 
     lax.fori_loop(0, 4, turn, 0)
+    ln.finish(gathered)
+    ln.finish(staged)
 
     for k in range(5):
         for red in reduces:
@@ -403,6 +425,7 @@
     for red in reduces:
         red.second()
     grads = [Gather(c, ln, x, axes) for x, (_, _, axes) in zip(Dx, PARTS)]
+    reduced = ln.taken()
     squares = jnp.zeros((8, 128), F32)
     for red, g, (_, width, _) in zip(reduces, grads, PARTS):
         res = red.third()
@@ -442,6 +465,7 @@
         first, width, axes = PARTS[i]
         if len(stages) == 0:
             sent = loss_send(2, "z", loss_wait(sent))
+            ln.finish(reduced)
         if len(stages) == 3:
             sent = loss_send(3, "dp", loss_wait(sent))
         stages.append(i)
@@ -469,7 +493,8 @@
 
     lax.fori_loop(0, 8, grad_step, 0)
     loss[...] = jnp.sum(loss_wait(sent), keepdims=True) / (TOKENS * D)
-    ln.finish()
+    ln.finish(ln.taken())
+    assert ln.n == RECEIVES and ln.batch == 4
 
 
 def placed(a, b, c, a_out, b_out, c_out, sems):
@@ -514,8 +539,8 @@
             pltpu.VMEM((2, 4, 2, ROWS, 128), F32),
             pltpu.VMEM((128, 128), F32),
             pltpu.VMEM((4, 4, 8, 128), F32),
-            pltpu.SemaphoreType.DMA((300,)),
-            pltpu.SemaphoreType.DMA((300,)),
+            pltpu.SemaphoreType.DMA((4,)),
+            pltpu.SemaphoreType.DMA((RECEIVES,)),
             pltpu.SemaphoreType.DMA((11,)),
         ],
         compiler_params=pltpu.CompilerParams(

time: 96.1 us -> 93.1 us (0.969)
  Pallas kernels: 91.4 us -> 88.3 us
    pallas_call x1, Pallas kernels: 89.4 us -> 86.4 us  [body(): pl.pallas_call(kernel, out_shape=(jax.ShapeDtypeStruct((D, SHID), BF16),...]
where the time goes in v3:
time: 93.1 us; the launch traced here: 92.9 us
  Pallas kernels  88.3 us (95%)
  between operations  2.4 us (3%)
  local copies, waits for them, and re-layouts  2.13 us (2%)
    pallas_call x1, Pallas kernels, body(): pl.pallas_call(kernel, out_shape=(jax.ShapeDtypeStruct((D, SHID), BF16),...  86.4 us
    unnamed x6, local copies, waits for them, and re-layouts  2.13 us
    pallas_call x1, Pallas kernels, body(): pl.pallas_call(placed, out_shape=tuple((jax.ShapeDtypeStruct(a.shape, BF1...  1.95 us

profile of v3, /device:TPU:1, one launch (start us, length us, event | category | flops | bytes accessed | tf_op | source)
XLA Modules:
  0.0 92.9 jit_solution(3684486266783716949)
XLA Ops:
  0.6 0.0 copy-start
  0.6 0.8 copy-done
  1.4 0.0 copy-start.1
  1.4 0.7 copy-done.1
  2.1 0.0 copy-start.2
  2.1 0.7 copy-done.2
  2.8 86.4 %shard_map.120 = (bf16[5120,128]{1,0:T(8,128)(2,1)S(1)}, bf16[5120,128]{1,0:T(8,128)(2,1)S(1)}, bf16[128,5120]{1,0:T(8,128)(2,1)S(1)}, f32[1,1]{1,0:T(1,128)}) custom-call(bf16[32,640]{1,0:T(8,128)(2,1)S(1)} %copy-done, s32[2,32]{1,0:T(2,128)S(1)} %bitcast.3, f32[2,32]{1,0:T(2,128)S(1)} %bitcast.4, bf16[1,5120,512]{2,1,0:T(8,128)(2,1)} %tg.1, ...), custom_call_target="tpu_custom_call" | custom-call | tf_op jit(solution)/shard_map/pallas_call | solution.py:512
  89.2 1.9 %shard_map.121 = (bf16[5120,128]{1,0:T(8,128)(2,1)}, bf16[5120,128]{1,0:T(8,128)(2,1)}, bf16[128,5120]{1,0:T(8,128)(2,1)}) custom-call(bf16[5120,128]{1,0:T(8,128)(2,1)S(1)} %get-tuple-element.11.a, bf16[5120,128]{1,0:T(8,128)(2,1)S(1)} %get-tuple-element.12.b, bf16[128,5120]{1,0:T(8,128)(2,1)S(1)} %get-tuple-element.13.c), custom_call_target="tpu_custom_call" | custom-call | tf_op jit(solution)/shard_map/pallas_call | solution.py:551
Async XLA Ops:
  0.6 0.8 copy-start
  1.4 0.7 copy-start.1
  2.1 0.7 copy-start.2

commit v4 on v3

--- a/solution.py
+++ b/solution.py
@@ -14,7 +14,7 @@
 D, ROWS, COLS, HID, SHID, TOKENS = 5120, 32, 640, 512, 128, 512
 PARTS = ((0, 256, "yzx"), (256, 256, "zxy"), (512, 128, "xyz"))
 GROUPS = (2, 3, 1, 0)
-RECEIVES = 241
+RECEIVES = 205
 F32, BF16 = jnp.float32, jnp.bfloat16
 
 
@@ -175,9 +175,9 @@
     def __init__(self, c, links, sums, got1, got2, got3, axes):
         self.c, self.ln, self.S, self.g1, self.g2, self.g3 = c, links, sums, got1, got2, got3
         self.a1, self.a2, self.a3 = axes
-        self.k1 = [[links.number() for _ in range(6)] for _ in range(4)]
-        self.k2 = [links.number() for _ in range(3)]
-        self.k3 = [links.number() for _ in range(3)]
+        first, second, third, fourth = ([links.number() for _ in range(4)] for _ in range(4))
+        self.k1 = [[first[k], second[k], second[k], third[k], fourth[k], fourth[k]] for k in range(4)]
+        self.k2, self.k3 = links.number(), links.number()
         self.r, self.l, self.o = (c[self.a3] + 1) % 4, (c[self.a3] + 3) % 4, (c[self.a3] + 2) % 4
 
     def idx(self, k, v3, rows=(0, ROWS)):
@@ -190,8 +190,10 @@
     def left(self, k, j, src):
         self.ln.send(src, self.g1.at[k, j], dev(self.a3, self.l), self.k1[k][j])
 
+    def arrived(self, k, j, n):
+        self.ln.wait(self.g1.at[k, pl.ds(j, n)], dev(self.a3, self.r if j < 3 else self.l), self.k1[k][j])
+
     def got(self, k, j):
-        self.ln.wait(self.g1.at[k, j], dev(self.a3, self.r if j < 3 else self.l), self.k1[k][j])
         return self.g1[k, j].astype(F32)
 
     def ring1(self, k):
@@ -204,14 +206,18 @@
     def ring2(self, k):
         S = self.S
         i = self.idx(k, self.r, (0, 16))
+        self.arrived(k, 0, 1)
         S[i] = (S[i].astype(F32) + self.got(k, 0)).astype(BF16)
         self.right(k, 2, S.at[i])
         i = self.idx(k, self.l, (16, 16))
+        self.arrived(k, 3, 1)
         S[i] = (S[i].astype(F32) + self.got(k, 3)).astype(BF16)
         self.left(k, 5, S.at[i])
 
     def ring3(self, k):
         S, own = self.S, self.c[self.a3]
+        self.arrived(k, 1, 2)
+        self.arrived(k, 4, 2)
         i = self.idx(k, own, (0, 16))
         S[i] = (S[i].astype(F32) + self.got(k, 4) + self.got(k, 2)).astype(BF16)
         i = self.idx(k, own, (16, 16))
@@ -219,24 +225,24 @@
         s = GROUPS[k]
         if s:
             to = dev(self.a2, self.c[self.a2] ^ s)
-            self.ln.send(S.at[self.idx(k, own)], self.g2.at[s - 1], to, self.k2[s - 1])
+            self.ln.send(S.at[self.idx(k, own)], self.g2.at[s - 1], to, self.k2)
 
     def second(self):
         S = self.S
         i = region(self.c, **{self.a1: None})
         total = S[i].astype(F32)
+        self.ln.wait(self.g2, dev(self.a2, self.c[self.a2] ^ 1), self.k2)
         for s in (1, 2, 3):
-            self.ln.wait(self.g2.at[s - 1], dev(self.a2, self.c[self.a2] ^ s), self.k2[s - 1])
             total = total + self.g2[s - 1].astype(F32)
         S[i] = total.astype(BF16)
         for s in (1, 3, 2):
             v1 = (self.c[self.a1] + s) % 4
-            self.ln.send(S.at[region(self.c, **{self.a1: v1})], self.g3.at[s - 1], dev(self.a1, v1), self.k3[s - 1])
+            self.ln.send(S.at[region(self.c, **{self.a1: v1})], self.g3.at[s - 1], dev(self.a1, v1), self.k3)
 
     def third(self):
         total = self.S[region(self.c)].astype(F32)
+        self.ln.wait(self.g3, dev(self.a1, (self.c[self.a1] + 1) % 4), self.k3)
         for s in (1, 2, 3):
-            self.ln.wait(self.g3.at[s - 1], dev(self.a1, (self.c[self.a1] + s) % 4), self.k3[s - 1])
             total = total + self.g3[s - 1].astype(F32)
         return total
 

time: 93.1 us -> 92.8 us (level)
  no operation moved by 1% of the time
where the time goes in v4:
time: 92.8 us; the launch traced here: 92.6 us
  Pallas kernels  88.1 us (95%)
  between operations  2.4 us (3%)
  local copies, waits for them, and re-layouts  2.13 us (2%)
    pallas_call x1, Pallas kernels, body(): pl.pallas_call(kernel, out_shape=(jax.ShapeDtypeStruct((D, SHID), BF16),...  86.1 us
    unnamed x6, local copies, waits for them, and re-layouts  2.13 us
    pallas_call x1, Pallas kernels, body(): pl.pallas_call(placed, out_shape=tuple((jax.ShapeDtypeStruct(a.shape, BF1...  1.95 us

profile of v4, /device:TPU:1, one launch (start us, length us, event | category | flops | bytes accessed | tf_op | source)
XLA Modules:
  0.0 92.6 jit_solution(923868244658768609)
XLA Ops:
  0.6 0.0 copy-start
  0.6 0.8 copy-done
  1.4 0.0 copy-start.1
  1.4 0.7 copy-done.1
  2.1 0.0 copy-start.2
  2.1 0.7 copy-done.2
  2.8 86.1 %shard_map.120 = (bf16[5120,128]{1,0:T(8,128)(2,1)S(1)}, bf16[5120,128]{1,0:T(8,128)(2,1)S(1)}, bf16[128,5120]{1,0:T(8,128)(2,1)S(1)}, f32[1,1]{1,0:T(1,128)}) custom-call(bf16[32,640]{1,0:T(8,128)(2,1)S(1)} %copy-done, s32[2,32]{1,0:T(2,128)S(1)} %bitcast.3, f32[2,32]{1,0:T(2,128)S(1)} %bitcast.4, bf16[1,5120,512]{2,1,0:T(8,128)(2,1)} %tg.1, ...), custom_call_target="tpu_custom_call" | custom-call | tf_op jit(solution)/shard_map/pallas_call | solution.py:518
  88.9 1.9 %shard_map.121 = (bf16[5120,128]{1,0:T(8,128)(2,1)}, bf16[5120,128]{1,0:T(8,128)(2,1)}, bf16[128,5120]{1,0:T(8,128)(2,1)}) custom-call(bf16[5120,128]{1,0:T(8,128)(2,1)S(1)} %get-tuple-element.11.a, bf16[5120,128]{1,0:T(8,128)(2,1)S(1)} %get-tuple-element.12.b, bf16[128,5120]{1,0:T(8,128)(2,1)S(1)} %get-tuple-element.13.c), custom_call_target="tpu_custom_call" | custom-call | tf_op jit(solution)/shard_map/pallas_call | solution.py:557
Async XLA Ops:
  0.6 0.8 copy-start
  1.4 0.7 copy-start.1
  2.1 0.7 copy-start.2
